TPU v7x, 256 devices: a whole 4x4x8 slice. The times are simulated.
256 devices in a mesh: head: 4 (over x_hi, core), inner: 16 (over x_lo, z), outer: 4 (over y).
Axes of the slice: x: 4 (x_hi: 2, x_lo: 2; x = x_hi * 2 + x_lo), y: 4, z: 8, core: 2. Of those that a mesh axis runs over, the one named last changes fastest.
Arguments:
- queries: bfloat16 [14336, 4096], P(('head', 'inner', 'outer')), may hold values from -400 to 400
- keys: bfloat16 [14336, 1024], P(('head', 'inner', 'outer')), may hold values from -14 to 14
- values: bfloat16 [14336, 1024], P(('head', 'inner', 'outer')), may hold values from -6 to 6
- span_order: int32 [256], replicated, may hold values from 0 to 255, each once
- block_pattern: int32 [256, 256], replicated, may hold values 0 or 1
- summary_flag: int32 [256], replicated, may hold values 0 or 1
Outputs:
- attended: bfloat16 [14336, 4096], P(('head', 'inner', 'outer'))
All inputs are finite; a program needn't handle non-finite values.
Results may differ from a plain program's by a relative error of at most 0.0064.
Values may be sent and summed in bfloat16 or wider, within the bound.
No kernel may reach another device: no remote copies, remote signals or barrier semaphores. Data moves between devices by JAX's collectives and lax.ppermute only.
A program may use at most 64 MiB of HBM per device.

v0:
```python
import math

import jax
import jax.numpy as jnp
from jax import lax
from jax.sharding import PartitionSpec as P

HEAD_SIZE = 128


NEG = -1e30
SCAN_LIMIT = 1024


def key_layout(piece_start, piece_rows, shard_rows, plain_rows, seq_count, order_table, span_rows):
    global_rows = piece_start + jnp.arange(piece_rows, dtype=jnp.int32)
    shard_index = global_rows // shard_rows
    within_shard = global_rows % shard_rows
    is_summary = within_shard >= plain_rows
    head_block = jnp.where(is_summary, within_shard - plain_rows, within_shard // span_rows)
    stored_span = head_block * seq_count + shard_index
    true_span = jnp.take(order_table, stored_span)
    position = true_span * span_rows + within_shard % span_rows
    return (is_summary, true_span, position)


def make_fold(
    query_heads,
    query_span,
    query_pos,
    full_ok,
    summary_ok,
    shard_rows,
    plain_rows,
    seq_count,
    order_table,
    span_rows,
    summary_bias,
):
    score_scale = 1.0 / math.sqrt(query_heads.shape[3])
    kv_heads = query_heads.shape[1]

    def one_block(state_carry, block_keys, block_values, piece_start):
        row_peak, row_total, weighted = state_carry
        piece_rows = block_keys.shape[0]
        is_summary, true_span, position = key_layout(
            piece_start, piece_rows, shard_rows, plain_rows, seq_count, order_table, span_rows
        )
        same_span = (query_span[:, None] == true_span[None, :]) & (
            position[None, :] <= query_pos[:, None]
        )
        full_allowed = jnp.take(full_ok, true_span, axis=1) > 0.5
        summary_allowed = jnp.take(summary_ok, true_span, axis=1) > 0.5
        allowed = jnp.where(is_summary[None, :], summary_allowed, same_span | full_allowed)
        extra_bias = jnp.where(is_summary, summary_bias, 0.0)
        key_heads = block_keys.reshape(piece_rows, kv_heads, -1)
        value_heads = block_values.reshape(piece_rows, kv_heads, -1)
        scores = (
            jnp.einsum("qhgd,khd->qhgk", query_heads, key_heads, preferred_element_type=jnp.float32)
            * score_scale
            + extra_bias
        )
        mask_wide = allowed[:, None, None, :]
        scores = jnp.where(mask_wide, scores, NEG)
        new_peak = jnp.maximum(row_peak, scores.max(-1))
        weights = jnp.where(mask_wide, jnp.exp(scores - new_peak[..., None]), 0.0)
        factor = jnp.exp(row_peak - new_peak)
        row_total = row_total * factor + weights.sum(-1)
        weighted = weighted * factor[..., None] + jnp.einsum(
            "qhgk,khd->qhgd",
            weights.astype(jnp.bfloat16),
            value_heads,
            preferred_element_type=jnp.float32,
        )
        return (new_peak, row_total, weighted)

    def fold_block(state_carry, kv_piece, piece_start):
        piece_keys, piece_values = kv_piece
        piece_rows = piece_keys.shape[0]
        if piece_rows > SCAN_LIMIT and piece_rows % shard_rows == 0:

            def inner_step(inner_carry, step_index):
                sub_keys = lax.dynamic_slice_in_dim(
                    piece_keys, step_index * shard_rows, shard_rows, 0
                )
                sub_values = lax.dynamic_slice_in_dim(
                    piece_values, step_index * shard_rows, shard_rows, 0
                )
                return (one_block(inner_carry, sub_keys, sub_values, step_index * shard_rows), None)

            state_carry, unused = lax.scan(
                inner_step, state_carry, jnp.arange(piece_rows // shard_rows, dtype=jnp.int32)
            )
            return state_carry
        return one_block(state_carry, piece_keys, piece_values, piece_start)

    return fold_block


def per_device(queries, keys, values, span_order, block_pattern, summary_flag):
    local_q, local_keys, local_values = (
        lax.all_to_all(queries, "head", split_axis=1, concat_axis=0, tiled=True),
        lax.all_to_all(keys, "head", split_axis=1, concat_axis=0, tiled=True),
        lax.all_to_all(values, "head", split_axis=1, concat_axis=0, tiled=True),
    )
    groups = lax.axis_size("head")
    seq_count = lax.axis_size(("inner", "outer"))
    seq_index = lax.axis_index(("inner", "outer"))
    span_rows = queries.shape[0]
    query_rows = local_q.shape[0]
    kv_heads = local_keys.shape[1] // HEAD_SIZE
    q_heads = local_q.shape[1] // HEAD_SIZE
    group_ratio = q_heads // kv_heads
    spans = span_order.shape[0]
    stored_span = jnp.arange(groups, dtype=jnp.int32) * seq_count + seq_index
    my_spans = jnp.take(span_order, stored_span)
    span_ids = jnp.arange(spans, dtype=jnp.int32)
    span_pick = (my_spans[:, None] == span_ids[None, :]).astype(jnp.float32)
    pattern_rows = jnp.dot(
        span_pick, block_pattern.astype(jnp.float32), preferred_element_type=jnp.float32
    )
    earlier = span_ids[None, :] < my_spans[:, None]
    flag_rows = (summary_flag == 1)[None, :]
    full_small = (earlier & (pattern_rows > 0.5)).astype(jnp.float32)
    summary_small = (earlier & (pattern_rows < 0.5) & flag_rows).astype(jnp.float32)
    full_ok = jnp.repeat(full_small, span_rows, axis=0)
    summary_ok = jnp.repeat(summary_small, span_rows, axis=0)
    query_span = jnp.repeat(my_spans, span_rows)
    query_pos = query_span * span_rows + jnp.arange(query_rows, dtype=jnp.int32) % span_rows
    query_heads = local_q.reshape(query_rows, kv_heads, group_ratio, HEAD_SIZE)
    summary_bias = math.log(span_rows)
    key_summary_sum = (
        jnp.sum(local_keys.reshape(groups, span_rows, -1), axis=1, dtype=jnp.float32)
        / math.sqrt(span_rows)
    ).astype(jnp.bfloat16)
    value_summary_sum = (
        jnp.sum(local_values.reshape(groups, span_rows, -1), axis=1, dtype=jnp.float32)
        / math.sqrt(span_rows)
    ).astype(jnp.bfloat16)
    shard_rows = local_keys.shape[0]
    fold_keys = make_fold(
        query_heads,
        query_span,
        query_pos,
        full_ok,
        summary_ok,
        shard_rows,
        query_rows,
        seq_count,
        span_order,
        span_rows,
        summary_bias,
    )
    start_state = (
        jnp.full((query_rows, kv_heads, group_ratio), NEG, jnp.float32),
        jnp.zeros((query_rows, kv_heads, group_ratio), jnp.float32),
        jnp.zeros((query_rows, kv_heads, group_ratio, HEAD_SIZE), jnp.float32),
    )
    state_carry = fold_keys(
        start_state,
        (
            lax.all_gather(local_keys, ("inner", "outer"), axis=0, tiled=True),
            lax.all_gather(local_values, ("inner", "outer"), axis=0, tiled=True),
        ),
        jnp.int32(0),
    )
    fold_summary = make_fold(
        query_heads,
        query_span,
        query_pos,
        full_ok,
        summary_ok,
        groups,
        0,
        seq_count,
        span_order,
        span_rows,
        summary_bias,
    )
    state_carry = fold_summary(
        state_carry,
        (
            lax.all_gather(key_summary_sum, ("inner", "outer"), axis=0, tiled=True),
            lax.all_gather(value_summary_sum, ("inner", "outer"), axis=0, tiled=True),
        ),
        jnp.int32(0),
    )
    row_peak, row_total, weighted = state_carry
    mixed = (
        (weighted / row_total[..., None])
        .reshape(query_rows, q_heads * HEAD_SIZE)
        .astype(jnp.bfloat16)
    )
    return lax.all_to_all(mixed, "head", split_axis=0, concat_axis=1, tiled=True)


def solution(mesh):
    return jax.shard_map(
        per_device,
        mesh=mesh,
        in_specs=(
            P(("head", "inner", "outer"), None),
            P(("head", "inner", "outer"), None),
            P(("head", "inner", "outer"), None),
            P(),
            P(),
            P(),
        ),
        out_specs=P(("head", "inner", "outer"), None),
        check_vma=False,
    )
```

profile of v0, /device:TPU:1, one launch (start us, length us, event | category | flops | bytes accessed | tf_op | source)
XLA Modules:
  0.0 1228.5 jit_solution(14990958466587590763)
XLA Ops:
  7.5 11.2 all_to_all.70
  19.7 9.0 all_to_all.71
  30.6 4.4 all-to-all-start.1
  35.0 1.9 gather_fusion.4
  40.9 133.6 %all-gather.1 = bf16[64,4,256]{2,1,0:T(4,128)(2,1)S(1)} all-gather(bf16[1,4,256]{2,1,0:T(4,128)(2,1)S(1)} %fusion.47), channel_id=1, replica_groups=mesh['head'=4,'inner'=16,'outer'=4] {'inner','outer'}, dimensions={0}, use_global_device_ids=true | all-gather | bytes 133120 | tf_op jit(solution)/shard_map/all_gather | solution.py:184
  174.6 127.0 %all-gather = bf16[64,4,256]{2,1,0:T(4,128)(2,1)S(1)} all-gather(bf16[1,4,256]{2,1,0:T(4,128)(2,1)S(1)} %fusion.46), channel_id=1, replica_groups=mesh['head'=4,'inner'=16,'outer'=4] {'inner','outer'}, dimensions={0}, use_global_device_ids=true | all-gather | bytes 133120 | tf_op jit(solution)/shard_map/all_gather | solution.py:183
  303.7 295.2 %all-gather.7.cloned.1.call-done = bf16[14336,256]{1,0:T(8,128)(2,1)} async-done(((bf16[224,256]{1,0:T(8,128)(2,1)}), bf16[14336,256]{1,0:T(8,128)(2,1)}) %all-gather.7.cloned.1.call-update) | async-done | bytes 7340048 | tf_op jit(solution)/shard_map/all_gather | solution.py:163
  598.9 563.0 %while.20 = (s32[]{:T(128)}, f32[224,2,4]{0,2,1:T(4,128)S(1)}, f32[224,2,4]{0,2,1:T(4,128)S(1)}, f32[224,2,4,128]{3,0,2,1:T(8,128)S(1)}, s32[64]{0:T(128)S(1)}, ...) while((s32[]{:T(128)}, f32[224,2,4]{0,2,1:T(4,128)S(1)}, ...), condition=%wide.region_3.5_spmd.clone.clone.clone, body=%wide.region_0.4_spmd.clone.clone.clone.sunk | while | flops 210708768 | bytes 11192455 | solution.py:91
  600.4 1.9 gather_fusion
  609.2 1.9 gather_fusion
  618.0 1.9 gather_fusion
  626.8 1.9 gather_fusion
  635.6 1.9 gather_fusion
  644.4 1.9 gather_fusion
  653.2 1.9 gather_fusion
  661.9 1.9 gather_fusion
  670.7 1.9 gather_fusion
  679.5 1.9 gather_fusion
  688.3 1.9 gather_fusion
  697.1 1.9 gather_fusion
  705.9 1.9 gather_fusion
  714.7 1.9 gather_fusion
  723.5 1.9 gather_fusion
  732.3 1.9 gather_fusion
  741.1 1.9 gather_fusion
  749.9 1.9 gather_fusion
  758.7 1.9 gather_fusion
  767.5 1.9 gather_fusion
  776.3 1.9 gather_fusion
  785.1 1.9 gather_fusion
  1161.9 2.3 fusion.26
  1165.8 55.1 %all_to_all.72 = bf16[4,56,1024]{2,1,0:T(8,128)(2,1)S(1)} all-to-all(bf16[4,56,1024]{2,1,0:T(8,128)(2,1)S(1)} %convert_element_type.48), channel_id=1, replica_groups=mesh['head'=4,'inner'=16,'outer'=4] {'head'}, dimensions={0} | all-to-all | bytes 917504 | tf_op jit(solution)/shard_map/all_to_all | solution.py:194
  (1769 shorter events, 482.4 us)
Async XLA Ops:
  6.5 28.5 %copy-start = (s32[256]{0:T(256)S(1)}, s32[256]{0:T(256)}, u32[]{:S(2)}) copy-start(s32[256]{0:T(256)} %param.15) | copy-start | bytes 3076
  6.5 297.2 %all-gather.5.cloned.1.call-start = ((), (), s32[]{:S(2)}) async-start(), calls=%async_computation.4 | async-start | bytes 7454720 | tf_op jit(solution)/shard_map/all_gather | solution.py:162
  18.7 580.2 %all-gather.7.cloned.1.call-start = ((), (), s32[]{:S(2)}) async-start(), calls=%async_computation.5 | async-start | bytes 7454720 | tf_op jit(solution)/shard_map/all_gather | solution.py:163
  28.7 9.2 copy-start.5
  28.7 9.2 copy-start.4
  30.6 271.0 %all-to-all-start.1 = ((bf16[56,4,1024]{2,0,1:T(8,128)(2,1)}), bf16[56,4,1024]{2,0,1:T(8,128)(2,1)S(1)}, u32[]{:S(2)}, u32[]{:S(2)}) async-start(bf16[56,4,1024]{2,0,1:T(8,128)(2,1)} %bitcast.75), calls=%async_computation.1 | async-start | bytes 917504 | tf_op jit(solution)/shard_map/all_to_all | solution.py:102
  39.4 1.4 copy-start.2
  39.4 1.4 copy-start.3
  1161.9 2.3 copy-start.1
Sparse Core Ops, SparseCore 0:
  18.8 270.2 all-gather.4
  291.0 307.8 all-gather.6
where the time goes:
time: 1230 us
  local copies, waits for them, and re-layouts  386 us (31%)
  blocking collectives  336 us (27%)
  waiting for transfers between devices  295 us (24%)
  matrix products  93.4 us (8%)
  other arithmetic  50.2 us (4%)
  loops' own time  49.8 us (4%)
  between operations  13.7 us (1%)
    all_gather x1, waiting for transfers between devices, per_device(): lax.all_gather(local_values, ('inner', 'outer'), axis=0, tiled=True)  295 us
    all_gather x1, blocking collectives, per_device(): lax.all_gather(value_summary_sum, ('inner', 'outer'), axis=0, tiled=True)  134 us
    all_gather x1, blocking collectives, per_device(): lax.all_gather(key_summary_sum, ('inner', 'outer'), axis=0, tiled=True)  127 us
    gather x65, local copies, waits for them, and re-layouts, key_layout(): true_span = jnp.take(order_table, stored_span)  127 us
    dynamic_slice x64, local copies, waits for them, and re-layouts, inner_step(): lax.dynamic_slice_in_dim(piece_values, step_index * shard_rows, shard_row...  62.6 us
    gather x65, local copies, waits for them, and re-layouts, one_block(): full_allowed = jnp.take(full_ok, true_span, axis=1) > 0.5  59.7 us
    gather x65, local copies, waits for them, and re-layouts, one_block(): summary_allowed = jnp.take(summary_ok, true_span, axis=1) > 0.5  59.7 us
    dot_general x65, matrix products, one_block(): jnp.einsum('qhgk,khd->qhgd', weights.astype(jnp.bfloat16), value_heads, p...  55.3 us
  transfers between devices with their start and end apart: 3, of which 1 were waited for; matrix products, arithmetic and copies ran while one was open for 1% of the time, Pallas kernels for 0%

commit v1 on v0

v1 whole, which is shorter than its diff:
```python
import math

import jax
import jax.numpy as jnp
from jax import lax
from jax.experimental import pallas as pl
from jax.experimental.pallas import tpu as pltpu
from jax.sharding import Mesh
from jax.sharding import PartitionSpec as P

HEAD = 128
GROUP = 4
SPAN = 56
PADDED = 64
ROWS = GROUP * SPAN
EXTRA = 16
BATCH = 4
NEG = -1e30
LOG2E = math.log2(math.e)
SCORE_SCALE = LOG2E / math.sqrt(HEAD)
SUMMARY_BIAS = math.log2(SPAN)

ROW = ("xhi", "core", "xlo")
ALL = ROW + ("z", "y")


def nt_dot(a, b):
    return lax.dot_general(a, b, (((1,), (1,)), ((), ())), preferred_element_type=jnp.float32)


def attend_kernel(list_ref, count_ref, own_ref, q_ref, kv_ref, bias_ref, out_ref, padded, sums, base, held):
    key_spans = kv_ref.shape[0]
    query_spans = q_ref.shape[0]
    gap = jnp.zeros((PADDED - SPAN, 2 * HEAD), jnp.bfloat16)

    def prepare(j, carry):
        block = kv_ref[j]
        padded[j] = jnp.concatenate([block, gap], axis=0)
        sums[pl.ds(j, 1), :] = jnp.sum(block.astype(jnp.float32), axis=0, keepdims=True)
        return carry

    lax.fori_loop(0, key_spans, prepare, 0)
    summary = (sums[...] / math.sqrt(SPAN)).astype(jnp.bfloat16)
    summary_keys = summary[:, :HEAD]
    summary_values = summary[:, HEAD:]

    base_cols = key_spans + PADDED
    row = lax.broadcasted_iota(jnp.int32, (ROWS, base_cols), 0) % SPAN
    col = lax.broadcasted_iota(jnp.int32, (ROWS, base_cols), 1) - key_spans
    causal = jnp.where((col >= 0) & (col <= row), 0.0, NEG)
    base_col = lax.broadcasted_iota(jnp.int32, (1, base_cols), 1)
    batch_col = lax.broadcasted_iota(jnp.int32, (1, BATCH * PADDED), 1)
    in_span = batch_col % PADDED < SPAN
    batch_slot = batch_col // PADDED
    pick = (
        lax.broadcasted_iota(jnp.int32, (8, HEAD), 0) == lax.broadcasted_iota(jnp.int32, (8, HEAD), 1)
    ).astype(jnp.bfloat16)
    lane = lax.broadcasted_iota(jnp.int32, (ROWS, HEAD), 1)

    def fold(x):
        return [x[:, k * HEAD : (k + 1) * HEAD] for k in range(x.shape[1] // HEAD)]

    def one_span(s, carry):
        count = count_ref[s]
        own = own_ref[s]
        batches = (count + BATCH - 1) // BATCH
        q = q_ref[s]
        own_block = padded[jnp.maximum(own, 0)]
        base_keys = jnp.concatenate([summary_keys, own_block[:, :HEAD]], axis=0)
        base_values = jnp.concatenate([summary_values, own_block[:, HEAD:]], axis=0)
        own_bias = jnp.where(own >= 0, 0.0, NEG)
        row_bias = jnp.where(base_col < key_spans, bias_ref[pl.ds(s, 1), :], own_bias)
        scores = nt_dot(q, base_keys) * SCORE_SCALE + jnp.where(base_col < key_spans, 0.0, causal) + row_bias
        base[...] = scores
        peak = fold(scores)
        peak = jnp.max(jnp.stack(peak), axis=0) if len(peak) > 1 else peak[0]

        def slots(t):
            blocks = [padded[list_ref[s, t * BATCH + k]] for k in range(BATCH)]
            return jnp.concatenate(blocks, axis=0)

        def score(t, peak):
            keys = slots(t)[:, :HEAD]
            ok = in_span & (batch_slot < count - t * BATCH)
            scores = nt_dot(q, keys) * SCORE_SCALE + jnp.where(ok, 0.0, NEG)
            held[t] = scores
            for part in fold(scores):
                peak = jnp.maximum(peak, part)
            return peak

        peak = lax.fori_loop(0, batches, score, peak)
        peak = jnp.max(peak, axis=1, keepdims=True)

        weight = jnp.exp2(base[...] - peak)
        total = sum(fold(weight))
        mixed = jnp.dot(weight.astype(jnp.bfloat16), base_values, preferred_element_type=jnp.float32)

        def mix(t, state):
            total, mixed = state
            weight = jnp.exp2(held[t] - peak)
            for part in fold(weight):
                total = total + part
            mixed = mixed + jnp.dot(
                weight.astype(jnp.bfloat16), slots(t)[:, HEAD:], preferred_element_type=jnp.float32
            )
            return total, mixed

        total, mixed = lax.fori_loop(0, batches, mix, (total, mixed))
        total = jnp.sum(total, axis=1, keepdims=True)
        out_ref[s, :ROWS, :] = (mixed / total).astype(jnp.bfloat16)
        level = peak + jnp.log2(total)
        high = level.astype(jnp.bfloat16).astype(jnp.float32)
        middle = (level - high).astype(jnp.bfloat16).astype(jnp.float32)
        low = level - high - middle
        parts = jnp.where(lane == 0, high, jnp.where(lane == 1, middle, jnp.where(lane == 2, low, 0.0)))
        flat = nt_dot(pick, parts.astype(jnp.bfloat16))
        tail = jnp.concatenate([flat[:, HEAD:], jnp.zeros((8, 2 * HEAD - ROWS), jnp.float32)], axis=1)
        out_ref[s, ROWS:, :] = jnp.concatenate([flat[:, :HEAD], tail], axis=0).astype(jnp.bfloat16)
        return carry

    lax.fori_loop(0, query_spans, one_span, 0)


def attend(lists, counts, owns, q, kv, bias):
    query_spans, key_spans = q.shape[0], kv.shape[0]
    vmem = pl.BlockSpec(memory_space=pltpu.VMEM)
    smem = pl.BlockSpec(memory_space=pltpu.SMEM)
    return pl.pallas_call(
        attend_kernel,
        out_shape=jax.ShapeDtypeStruct((query_spans, ROWS + EXTRA, HEAD), jnp.bfloat16),
        in_specs=[smem, smem, smem, vmem, vmem, vmem],
        out_specs=vmem,
        scratch_shapes=[
            pltpu.VMEM((key_spans, PADDED, 2 * HEAD), jnp.bfloat16),
            pltpu.VMEM((key_spans, 2 * HEAD), jnp.float32),
            pltpu.VMEM((ROWS, key_spans + PADDED), jnp.float32),
            pltpu.VMEM((key_spans // BATCH, ROWS, BATCH * PADDED), jnp.float32),
        ],
        compiler_params=pltpu.CompilerParams(vmem_limit_bytes=40 * 1024 * 1024),
    )(lists, counts, owns, q, kv, bias)


def combine_kernel(parts_ref, out_ref, *, pieces):
    heads = parts_ref.shape[0] // pieces
    three = (lax.broadcasted_iota(jnp.int32, (8, HEAD), 0) < 3).astype(jnp.bfloat16)

    def spread(rows):
        return lax.dot_general(rows, three, (((0,), (0,)), ((), ())), preferred_element_type=jnp.float32)

    for h in range(heads):
        levels = []
        for y in range(pieces):
            tail = parts_ref[h * pieces + y, ROWS:, :].astype(jnp.float32)
            both = [spread(tail[k * 8 : k * 8 + 8].astype(jnp.bfloat16)) for k in range(2)]
            levels.append(jnp.concatenate(both, axis=0)[:ROWS])
        peak = levels[0]
        for level in levels[1:]:
            peak = jnp.maximum(peak, level)
        total = jnp.zeros_like(peak)
        mixed = jnp.zeros_like(peak)
        for y in range(pieces):
            weight = jnp.exp2(levels[y] - peak)
            total = total + weight
            mixed = mixed + weight * parts_ref[h * pieces + y, :ROWS, :].astype(jnp.float32)
        mixed = (mixed / total)
        for g in range(GROUP):
            at = (h * GROUP + g) * HEAD
            out_ref[:, at : at + HEAD] = mixed[g * SPAN : (g + 1) * SPAN].astype(jnp.bfloat16)


def combine(parts, pieces):
    heads = parts.shape[0] // pieces
    vmem = pl.BlockSpec(memory_space=pltpu.VMEM)

    def kernel(parts_ref, out_ref):
        combine_kernel(parts_ref, out_ref, pieces=pieces)

    return pl.pallas_call(
        kernel,
        out_shape=jax.ShapeDtypeStruct((SPAN, heads * GROUP * HEAD), jnp.bfloat16),
        in_specs=[vmem],
        out_specs=vmem,
        compiler_params=pltpu.CompilerParams(vmem_limit_bytes=32 * 1024 * 1024),
    )(parts)


def tables(query_true, key_true, block_pattern, summary_flag):
    spans = block_pattern.shape[0]
    ids = jnp.arange(spans, dtype=jnp.int32)
    query_pick = (query_true[:, None] == ids[None, :]).astype(jnp.bfloat16)
    key_pick = (key_true[:, None] == ids[None, :]).astype(jnp.bfloat16)
    rows = jnp.dot(query_pick, block_pattern.astype(jnp.bfloat16), preferred_element_type=jnp.float32)
    pattern = nt_dot(rows.astype(jnp.bfloat16), key_pick) > 0.5
    flag = nt_dot((summary_flag == 1).astype(jnp.bfloat16)[None, :], key_pick) > 0.5
    earlier = key_true[None, :] < query_true[:, None]
    full = earlier & pattern
    bias = jnp.where(earlier & ~pattern & flag, SUMMARY_BIAS, NEG).astype(jnp.float32)
    slot = jnp.arange(key_true.shape[0], dtype=jnp.int32)
    upto = (slot[:, None] <= slot[None, :]).astype(jnp.bfloat16)
    rank = jnp.dot(full.astype(jnp.bfloat16), upto, preferred_element_type=jnp.float32).astype(jnp.int32) - 1
    hit = full[:, None, :] & (rank[:, None, :] == slot[None, :, None])
    lists = jnp.sum(jnp.where(hit, slot[None, None, :], 0), axis=2, dtype=jnp.int32)
    counts = jnp.sum(full.astype(jnp.int32), axis=1, dtype=jnp.int32)
    same = key_true[None, :] == query_true[:, None]
    owns = jnp.sum(jnp.where(same, slot[None, :] + 1, 0), axis=1, dtype=jnp.int32) - 1
    bias = jnp.concatenate([bias, jnp.full((bias.shape[0], PADDED), NEG, jnp.float32)], axis=1)
    return lists, counts, owns, bias


def per_device(queries, keys, values, span_order, block_pattern, summary_flag):
    heads = keys.shape[1] // HEAD
    pieces = lax.axis_size("y")
    by_head = [x.reshape(SPAN, heads, HEAD).transpose(1, 0, 2) for x in (keys, values)]
    kv = jnp.concatenate(by_head, axis=2)
    kv = lax.all_to_all(kv, ROW, split_axis=0, concat_axis=0, tiled=True)
    kv = lax.all_gather(kv, "z", axis=0, tiled=True)

    q = queries.reshape(SPAN, heads, GROUP, HEAD).transpose(1, 2, 0, 3).reshape(heads, 1, ROWS, HEAD)
    q = jnp.broadcast_to(q, (heads, pieces, ROWS, HEAD)).reshape(heads * pieces, ROWS, HEAD)
    q = lax.all_to_all(q, ROW + ("y",), split_axis=0, concat_axis=0, tiled=True)

    order = span_order.reshape(heads, lax.axis_size("z"), pieces)
    query_true = lax.dynamic_index_in_dim(order, lax.axis_index("z"), 1, keepdims=False).reshape(-1)
    key_true = lax.dynamic_index_in_dim(order, lax.axis_index("y"), 2, keepdims=False).T.reshape(-1)
    lists, counts, owns, bias = tables(query_true, key_true, block_pattern, summary_flag)
    parts = attend(lists, counts, owns, q, kv, bias)
    parts = lax.all_to_all(parts, ROW + ("y",), split_axis=0, concat_axis=0, tiled=True)
    return combine(parts, pieces)


def solution(mesh):
    fine = Mesh(mesh.devices.reshape(2, 2, 2, 8, 4), ALL)
    return jax.shard_map(
        per_device,
        mesh=fine,
        in_specs=(P(ALL, None), P(ALL, None), P(ALL, None), P(), P(), P()),
        out_specs=P(ALL, None),
        check_vma=False,
    )
```

time: 1230 us -> 148 us (0.12)
  local copies, waits for them, and re-layouts: 386 us -> 6.1 us
  blocking collectives: 336 us -> 48.9 us
  waiting for transfers between devices: 295 us -> 28 us
  matrix products: 93.4 us -> 0.76 us
  loops' own time: 49.8 us -> 0 us
  other arithmetic: 50.2 us -> 0.74 us
  Pallas kernels: 0 us -> 43.9 us
    all_gather x2 -> x1, waiting for transfers between devices: 295 us -> 5.36 us  [per_device(): kv = lax.all_gather(kv, 'z', axis=0, tiled=True)]
    all_gather x2 -> x0, blocking collectives: 261 us -> none  [the longest x1 134 us: per_device(): lax.all_gather(value_summary_sum, ('inner', 'outer'), axis=0, tiled=True)]
    gather x196 -> x0, local copies, waits for them, and re-layouts: 247 us -> none  [the longest x65 127 us: key_layout(): true_span = jnp.take(order_table, stored_span)]
    dynamic_slice x128 -> x2, local copies, waits for them, and re-layouts: 100 us -> 0.31 us  [the longest x1 0.28 us: per_device(): lax.dynamic_index_in_dim(order, lax.axis_index('y'), 2, keepdims=False)]
    dot_general x131 -> x3, matrix products: 93.4 us -> 0.76 us  [the longest x2 0.63 us: nt_dot(): lax.dot_general(a, b, (((1,), (1,)), ((), ())), preferred_element_type=jn...]
    another operation x1 -> x0, loops' own time: 49.8 us -> none  [fold_block(): lax.scan(inner_step, state_carry, jnp.arange(piece_rows // shard_rows, dt...]
    pallas_call x0 -> x2, Pallas kernels: none -> 43.9 us  [the longest x1 41.9 us: attend(): pl.pallas_call(attend_kernel, out_shape=jax.ShapeDtypeStruct((query_spans...]
    all_to_all x3 -> x2, blocking collectives: 75.4 us -> 48.9 us  [the longest x1 36.6 us: per_device(): lax.all_to_all(parts, ROW + ('y',), split_axis=0, concat_axis=0, tiled=True)]
  transfers between devices with their start and end apart: 3 -> 2, of which waited for: 1 -> 2; matrix products, arithmetic and copies ran while one was open for 1% -> 3% of each run, Pallas kernels for 0% -> 0%
where the time goes in v1:
time: 148 us
  blocking collectives  48.9 us (33%)
  Pallas kernels  43.9 us (30%)
  waiting for transfers between devices  28 us (19%)
  between operations  13.5 us (9%)
  local copies, waits for them, and re-layouts  6.1 us (4%)
  starting transfers between devices  5.94 us (4%)
    pallas_call x1, Pallas kernels, attend(): pl.pallas_call(attend_kernel, out_shape=jax.ShapeDtypeStruct((query_spans...  41.9 us
    all_to_all x1, blocking collectives, per_device(): lax.all_to_all(parts, ROW + ('y',), split_axis=0, concat_axis=0, tiled=True)  36.6 us
    all_to_all x1, waiting for transfers between devices, per_device(): q = lax.all_to_all(q, ROW + ('y',), split_axis=0, concat_axis=0, tiled=True)  22.6 us
    all_to_all x1, blocking collectives, per_device(): kv = lax.all_to_all(kv, ROW, split_axis=0, concat_axis=0, tiled=True)  12.3 us
    all_to_all x1, starting transfers between devices, per_device(): q = lax.all_to_all(q, ROW + ('y',), split_axis=0, concat_axis=0, tiled=True)  5.94 us
    all_gather x1, waiting for transfers between devices, per_device(): kv = lax.all_gather(kv, 'z', axis=0, tiled=True)  5.36 us
    unnamed x12, local copies, waits for them, and re-layouts  3.4 us
  transfers between devices with their start and end apart: 2, of which 2 were waited for; matrix products, arithmetic and copies ran while one was open for 3% of the time, Pallas kernels for 0%

profile of v1, /device:TPU:1, one launch (start us, length us, event | category | flops | bytes accessed | tf_op | source)
XLA Modules:
  0.0 147.9 jit_solution(4094776239920435315)
XLA Ops:
  6.5 0.0 copy-start.1
  6.5 0.0 all-gather.2.cloned.1.call-start
  6.5 1.0 copy.25
  7.5 0.9 copy.26
  8.5 12.3 %all_to_all.15 = bf16[8,56,256]{2,1,0:T(8,128)(2,1)} all-to-all(bf16[8,56,256]{2,1,0:T(8,128)(2,1)S(1)} %copy.24), channel_id=1, replica_groups=mesh['xhi'=2,'core'=2,'xlo'=2,'z'=8,'y'=4] {'xhi','core','xlo'}, dimensions={0} | all-to-all | bytes 458752 | tf_op jit(solution)/shard_map/all_to_all | solution.py:215
  20.8 0.0 all-gather.2.cloned.1.call-update
  20.9 0.0 copy-done.1
  20.9 0.3 reshape.34
  21.2 0.2 copy.23
  21.4 1.5 %broadcast_in_dim.55 = bf16[8,4,224,128]{3,2,1,0:T(8,128)(2,1)} broadcast(bf16[8,224,128]{2,1,0:T(8,128)(2,1)S(1)} %bitcast.21), dimensions={0,2,3} | broadcast | bytes 2293760 | tf_op jit(solution)/shard_map/broadcast_in_dim | solution.py:219
  22.9 0.0 copy-start.4
  22.9 0.0 copy-start.3
  22.9 5.9 %all-to-all-start = ((bf16[32,224,128]{2,1,0:T(8,128)(2,1)}), bf16[32,224,128]{2,1,0:T(8,128)(2,1)S(1)}, u32[]{:S(2)}, u32[]{:S(2)}) async-start(bf16[32,224,128]{2,1,0:T(8,128)(2,1)} %bitcast.19), calls=%async_computation | async-start | bytes 3670016 | tf_op jit(solution)/shard_map/all_to_all | solution.py:220
  28.8 0.0 copy-done.4
  28.9 0.0 copy-done.3
  28.9 0.1 reshape.33
  29.0 0.1 lt.29
  29.1 0.3 dynamic-slice_reduce_fusion
  29.4 0.1 copy.22
  29.5 0.1 lt.26
  29.6 0.2 fusion.3
  29.8 0.0 copy-done.2
  29.8 0.4 convert_reduce_fusion
  30.2 0.1 fusion.12
  30.3 0.1 fusion.1
  30.4 0.6 select_reduce_fusion.list_ref
  31.0 22.6 %all-to-all-done.q_ref = bf16[32,224,128]{2,1,0:T(8,128)(2,1)S(1)} async-done(((bf16[32,224,128]{2,1,0:T(8,128)(2,1)}), bf16[32,224,128]{2,1,0:T(8,128)(2,1)S(1)}, u32[]{:S(2)}, u32[]{:S(2)}) %all-to-all-start) | async-done | bytes 1835040 | tf_op jit(solution)/shard_map/all_to_all | solution.py:220
  53.7 5.4 %all-gather.2.cloned.1.call-done.kv_ref = bf16[64,56,256]{2,1,0:T(8,128)(2,1)} async-done(((bf16[8,56,256]{2,1,0:T(8,128)(2,1)}), bf16[64,56,256]{2,1,0:T(8,128)(2,1)}) %all-gather.2.cloned.1.call-update) | async-done | bytes 1835024 | tf_op jit(solution)/shard_map/all_gather | solution.py:216
  59.0 1.5 %copy-done = bf16[64,56,256]{2,1,0:T(8,128)(2,1)S(1)} copy-done((bf16[64,56,256]{2,1,0:T(8,128)(2,1)S(1)}, bf16[64,56,256]{2,1,0:T(8,128)(2,1)}, u32[]{:S(2)}) %copy-start) | copy-done | bytes 1835032
  60.5 41.9 %shard_map.64 = bf16[32,240,128]{2,1,0:T(8,128)(2,1)S(1)} custom-call(s32[32,64]{1,0:T(8,128)S(1)} %select_reduce_fusion.list_ref, s32[32]{0:T(128)S(1)} %get-tuple-element.5.count_ref, s32[32]{0:T(128)S(1)} %broadcast_add_fusion.own_ref, bf16[32,224,128]{2,1,0:T(8,128)(2,1)S(1)} %all-to-all-done.q_ref, bf16[64,56,256]{2,1,0:T(8,128)(2,1)S(1)} %copy-done, ...), custom_call_target="tpu_custom_call" | custom-call | tf_op jit(solution)/shard_map/pallas_call | solution.py:128
  102.5 36.6 %all_to_all.16.parts_ref = bf16[32,240,128]{2,1,0:T(8,128)(2,1)S(1)} all-to-all(bf16[32,240,128]{2,1,0:T(8,128)(2,1)S(1)} %shard_map.64), channel_id=1, replica_groups=mesh['xhi'=2,'core'=2,'xlo'=2,'z'=8,'y'=4] {'xhi','core','xlo','y'}, dimensions={0} | all-to-all | bytes 3932160 | tf_op jit(solution)/shard_map/all_to_all | solution.py:227
  139.1 2.0 %shard_map.65 = bf16[56,4096]{1,0:T(8,128)(2,1)} custom-call(bf16[32,240,128]{2,1,0:T(8,128)(2,1)S(1)} %all_to_all.16.parts_ref), custom_call_target="tpu_custom_call" | custom-call | tf_op jit(solution)/shard_map/pallas_call | solution.py:178
  (10 shorter events, 0.1 us)
Async XLA Ops:
  6.5 14.3 %copy-start.1 = (bf16[56,4096]{1,0:T(8,128)(2,1)S(1)}, bf16[56,4096]{1,0:T(8,128)(2,1)}, u32[]{:S(2)}) copy-start(bf16[56,4096]{1,0:T(8,128)(2,1)} %param.6) | copy-start | bytes 1376260
  6.5 52.5 %all-gather.2.cloned.1.call-start = ((), (), s32[]{:S(2)}) async-start(), calls=%async_computation.3 | async-start | bytes 2064384 | tf_op jit(solution)/shard_map/all_gather | solution.py:216
  22.9 6.0 %copy-start.4 = (s32[256]{0:T(256)S(1)}, s32[256]{0:T(256)}, u32[]{:S(2)}) copy-start(s32[256]{0:T(256)} %param.11) | copy-start | bytes 3076
  22.9 6.0 %copy-start.3 = (s32[256]{0:T(256)S(1)}, s32[256]{0:T(256)}, u32[]{:S(2)}) copy-start(s32[256]{0:T(256)} %param.9) | copy-start | bytes 3076
  22.9 6.9 %copy-start.2 = (s32[256,256]{1,0:T(8,128)S(1)}, s32[256,256]{1,0:T(8,128)}, u32[]{:S(2)}) copy-start(s32[256,256]{1,0:T(8,128)} %param.10) | copy-start | bytes 786436
  22.9 30.8 %all-to-all-start = ((bf16[32,224,128]{2,1,0:T(8,128)(2,1)}), bf16[32,224,128]{2,1,0:T(8,128)(2,1)S(1)}, u32[]{:S(2)}, u32[]{:S(2)}) async-start(bf16[32,224,128]{2,1,0:T(8,128)(2,1)} %bitcast.19), calls=%async_computation | async-start | bytes 3670016 | tf_op jit(solution)/shard_map/all_to_all | solution.py:220
  59.0 1.5 %copy-start = (bf16[64,56,256]{2,1,0:T(8,128)(2,1)S(1)}, bf16[64,56,256]{2,1,0:T(8,128)(2,1)}, u32[]{:S(2)}) copy-start(bf16[64,56,256]{2,1,0:T(8,128)(2,1)} %all-gather.2.cloned.1.call-done.kv_ref) | copy-start | bytes 5505028
Sparse Core Ops, SparseCore 0:
  21.0 37.9 all-gather.1
